TPU v7x, 1024 devices: a whole 8x8x8 slice. The times are simulated.
1024 devices in a mesh: row: 16 (over x, core), col: 64 (over z, y).
Axes of the slice: x: 8, y: 8, z: 8, core: 2. Of those that a mesh axis runs over, the one named last changes fastest.
Arguments:
- fwd_now: float32 [3, 8388608], P(None, ('row', 'col')), may hold values from -6 to 6
- fwd_prev: float32 [3, 8388608], P(None, ('row', 'col')), may hold values from -6 to 6
- adj_now: float32 [3, 8388608], P(None, ('row', 'col')), may hold values from -6 to 6
- adj_prev: float32 [3, 8388608], P(None, ('row', 'col')), may hold values from -6 to 6
- inv_mass: float32 [8388608], P(('row', 'col')), may hold values from 0.1 to 1
- ibool: int32 [125, 131072], P(None, ('row', 'col')), may hold values from 0 to 8191
- inv_jac: float32 [3, 131072], P(None, ('row', 'col')), may hold values from 0.5 to 1.5
- kappa: float32 [125, 131072], P(None, ('row', 'col')), may hold values from 0.5 to 2
- mu: float32 [125, 131072], P(None, ('row', 'col')), may hold values from 0.2 to 1
- elem_count: int32 [1024], P(('row', 'col')), may hold values from 1 to 128, 98304 in all
- face_nodes: int32 [1024, 4, 640], P(('row', 'col')), may hold values from 0 to 8191
- face_len: int32 [1024, 4], P(('row', 'col')), may hold values from 0 to 640, as said below
- edge_nodes: int32 [1024, 4, 42], P(('row', 'col')), may hold values from 0 to 8191
- edge_len: int32 [1024, 4], P(('row', 'col')), may hold values from 0 to 42, as said below
- rec_elem: int32 [131072], P(('row', 'col')), may hold values from 0 to 127
- adj_src: float32 [2, 3, 131072], P(None, None, ('row', 'col')), may hold values from -24 to 24
Outputs:
- fwd_out: float32 [3, 8388608], P(None, ('row', 'col'))
- adj_out: float32 [3, 8388608], P(None, ('row', 'col'))
- rho_kernel: float32 [125, 131072], P(None, ('row', 'col'))
- kappa_kernel: float32 [125, 131072], P(None, ('row', 'col'))
- mu_kernel: float32 [125, 131072], P(None, ('row', 'col'))
Inputs may be any that keep to these rules, and one draw needn't show every extreme that they name: face_len[p, s] equals the partner's length for the opposite slot, is 0 where the partner lies outside the grid and else at least 640 // 2; some pair along col has 640. edge_len[p, s] equals the partner's length for the opposite slot, is 0 where the partner lies outside the grid and else at least max(42 // 2, 1); some pair has 42.
All inputs are finite; a program needn't handle non-finite values. No bound on the sum of `elem_count` on one device may be relied on, other than what follows from the above.
Results may differ from a plain program's by a relative error of at most 0.0003.
Values sent between devices are 32-bit elements; how exact they have to be, the bound alone decides.
A program may use at most 128 MiB of HBM per device.

v0:
```python
import math

import jax
import jax.numpy as jnp
import numpy as np
from jax import lax
from jax.sharding import PartitionSpec as P

time_step = 0.5


def shifted(array, axis, by):
    size = lax.axis_size(axis)
    pairs = [(i, i + by) for i in range(size) if 0 <= i + by < size]
    return lax.ppermute(array, axis, pairs)


def gll_tables():
    points = np.array([-1.0, -math.sqrt(3.0 / 7.0), 0.0, math.sqrt(3.0 / 7.0), 1.0])
    weights = np.array([0.1, 49.0 / 90.0, 32.0 / 45.0, 49.0 / 90.0, 0.1])
    table = np.zeros((5, 5))
    for a in range(5):
        for i in range(5):
            if a != i:
                prod_a = np.prod([points[a] - points[m] for m in range(5) if m != a])
                prod_i = np.prod([points[i] - points[m] for m in range(5) if m != i])
                table[a, i] = prod_a / (prod_i * (points[a] - points[i]))
            else:
                table[a, a] = sum([1.0 / (points[a] - points[m]) for m in range(5) if m != a])
    cube = weights[:, None, None] * weights[None, :, None] * weights[None, None, :]
    return (table, cube)


def operator_stack():
    table, cube = gll_tables()
    ident_five = np.eye(5)
    along_x = np.kron(np.eye(25), table)
    along_y = np.kron(np.kron(ident_five, table), ident_five)
    along_z = np.kron(table, np.eye(25))
    stacked = np.concatenate([along_x, along_y, along_z], 0)
    return (jnp.asarray(stacked, jnp.float32), jnp.asarray(cube.reshape(125), jnp.float32))


def element_force(points_field, inv_jac, kappa, mu):
    stacked, cube = operator_stack()
    count = points_field.shape[-1]
    high = lax.Precision.HIGHEST
    scales = inv_jac[None, :, None, :]
    grads = (
        jnp.einsum("pq,cqe->cpe", stacked, points_field, precision=high).reshape(3, 3, 125, count)
        * scales
    )
    strain = 0.5 * (grads + jnp.swapaxes(grads, 0, 1))
    div = grads[0, 0] + grads[1, 1] + grads[2, 2]
    ident = jnp.eye(3, dtype=jnp.float32)[:, :, None, None]
    stress = 2.0 * mu * strain + (kappa - 2.0 / 3.0 * mu) * div * ident
    weight = cube[:, None] / (inv_jac[0] * inv_jac[1] * inv_jac[2])
    flux = (stress * weight * scales).reshape(3, 375, count)
    force = jnp.einsum("pq,cpe->cqe", stacked, flux, precision=high)
    deviator = strain - div / 3.0 * ident
    return (force, div, deviator)


def nodal_force(field, connect, inv_jac, kappa, mu, keep):
    points = field[:, connect]
    force, div, deviator = element_force(points, inv_jac, kappa, mu)
    nodes = jnp.zeros_like(field).at[:, connect].add(-force * keep)
    return (nodes, points, div, deviator)


def assemble(force, face_list, face_keep, edge_list, edge_keep):
    face_sent = force[:, face_list] * face_keep[None]
    edge_sent = force[:, edge_list] * edge_keep[None]
    got_face = [None, None, None, None]
    got_edge = [None, None, None, None]
    for sender, by, slot in ((0, 1, 1), (1, -1, 0)):
        got_face[slot] = shifted(face_sent[:, sender], "col", by)
    for sender, by, slot in ((2, 1, 3), (3, -1, 2)):
        got_face[slot] = shifted(face_sent[:, sender], "row", by)
    across = lax.axis_size("col")
    for sender, by, slot in (
        (0, across + 1, 3),
        (1, across - 1, 2),
        (2, 1 - across, 1),
        (3, -across - 1, 0),
    ):
        got_edge[slot] = shifted(edge_sent[:, sender], ("row", "col"), by)
    total = force.at[:, face_list].add(jnp.stack(got_face, 1))
    return total.at[:, edge_list].add(jnp.stack(got_edge, 1))


def on_device(
    fwd_now,
    fwd_prev,
    adj_now,
    adj_prev,
    inv_mass,
    ibool,
    inv_jac,
    kappa,
    mu,
    elem_count,
    face_nodes,
    face_len,
    edge_nodes,
    edge_len,
    rec_elem,
    adj_src,
):
    elements = ibool.shape[1]
    keep = (jnp.arange(elements) < elem_count[0]).astype(jnp.float32)
    face_list = face_nodes[0]
    edge_list = edge_nodes[0]
    face_keep = (jnp.arange(face_list.shape[1])[None, :] < face_len[0][:, None]).astype(jnp.float32)
    edge_keep = (jnp.arange(edge_list.shape[1])[None, :] < edge_len[0][:, None]).astype(jnp.float32)
    source_nodes = ibool[62][rec_elem]
    masses = inv_mass[None, :]
    rho_k = jnp.zeros((125, elements), jnp.float32)
    kappa_k = jnp.zeros((125, elements), jnp.float32)
    mu_k = jnp.zeros((125, elements), jnp.float32)
    forward, before_f = (fwd_now, fwd_prev)
    adjoint, before_a = (adj_now, adj_prev)
    for step in range(adj_src.shape[0]):
        local_f, points_f, div_f, dev_f = nodal_force(forward, ibool, inv_jac, kappa, mu, keep)
        total_f = assemble(local_f, face_list, face_keep, edge_list, edge_keep)
        local_a, points_a, div_a, dev_a = nodal_force(adjoint, ibool, inv_jac, kappa, mu, keep)
        local_a = local_a.at[:, source_nodes].add(adj_src[step])
        total_a = assemble(local_a, face_list, face_keep, edge_list, edge_keep)
        accel_a = masses * total_a
        rho_k = rho_k + time_step * jnp.sum(accel_a[:, ibool] * points_f, 0) * keep
        kappa_k = kappa_k + time_step * div_f * div_a * keep
        mu_k = mu_k + 2.0 * time_step * jnp.sum(dev_f * dev_a, (0, 1)) * keep
        next_f = 2.0 * forward - before_f + time_step * time_step * masses * total_f
        next_a = 2.0 * adjoint - before_a + time_step * time_step * masses * total_a
        before_f, forward = (forward, next_f)
        before_a, adjoint = (adjoint, next_a)
    return (forward, adjoint, rho_k, kappa_k, mu_k)


def solution(mesh):
    in_specs = (
        P(None, ("row", "col")),
        P(None, ("row", "col")),
        P(None, ("row", "col")),
        P(None, ("row", "col")),
        P(("row", "col")),
        P(None, ("row", "col")),
        P(None, ("row", "col")),
        P(None, ("row", "col")),
        P(None, ("row", "col")),
        P(("row", "col")),
        P(("row", "col"), None, None),
        P(("row", "col"), None),
        P(("row", "col"), None, None),
        P(("row", "col"), None),
        P(("row", "col")),
        P(None, None, ("row", "col")),
    )
    out_specs = (
        P(None, ("row", "col")),
        P(None, ("row", "col")),
        P(None, ("row", "col")),
        P(None, ("row", "col")),
        P(None, ("row", "col")),
    )
    return jax.shard_map(
        on_device, mesh=mesh, in_specs=in_specs, out_specs=out_specs, check_vma=False
    )
```

profile of v0, /device:TPU:1, one launch (start us, length us, event | category | flops | bytes accessed | tf_op | source)
XLA Modules:
  0.0 954.9 jit_solution(1135736612700746988)
XLA Ops:
  13.8 32.6 %gather_fusion = f32[16000,3]{1,0:T(8,128)} fusion(f32[3,8192]{0,1:T(8,128)} %copy.192, s32[16384]{0:T(1024)S(1)} %pad_clamp_fusion), kind=kCustom, calls=%fused_computation | custom fusion | bytes 448000 | tf_op jit(solution)/shard_map/gather | solution.py:65
  55.1 32.6 %gather_fusion.6 = f32[16000,3]{1,0:T(8,128)} fusion(f32[3,8192]{0,1:T(8,128)} %copy.223, s32[16384]{0:T(1024)S(1)} %pad_clamp_fusion), kind=kCustom, calls=%fused_computation.6 | custom fusion | bytes 448000 | tf_op jit(solution)/shard_map/gather | solution.py:65
  103.2 90.4 %scatter_custom_fusion = f32[3,8192]{0,1:T(8,128)} fusion(s32[16000]{0:T(1024)S(1)} %fusion.22, f32[16000,3]{1,0:T(8,128)} %bitcast.319, f32[]{:T(128)} %constant.13.clone.1), kind=kCustom, calls=%fused_computation.37 | custom fusion | flops 48000 | bytes 98816 | tf_op jit(solution)/shard_map/scatter-add | solution.py:67
  202.0 90.1 %scatter_custom_fusion.6 = f32[3,8192]{0,1:T(8,128)} fusion(s32[16000]{0:T(1024)S(1)} %fusion.22, f32[16000,3]{1,0:T(8,128)} %bitcast.320, f32[]{:T(128)} %constant.13.clone.1), kind=kCustom, calls=%fused_computation.33 | custom fusion | flops 48000 | bytes 98816 | tf_op jit(solution)/shard_map/scatter-add | solution.py:67
  305.5 18.8 %collective-permute-start.6 = (f32[3,42]{1,0:T(4,128)S(1)}, f32[3,42]{1,0:T(4,128)S(1)}, u32[]{:S(2)}, u32[]{:S(2)}) collective-permute-start(f32[3,42]{1,0:T(4,128)S(1)} %bitcast.350), channel_id=1, source_target_pairs={{0,63},{1,64},{2,65},{3,66},{4,67},{5,68},{6,69},{7,70},{8,71},{9,... | collective-permute-start | bytes 1520 | tf_op jit(solution)/shard_map/ppermute | solution.py:15
  328.9 7.8 gather_fusion.1
  336.8 6.3 gather_fusion.8
  346.7 8.9 collective-permute-start.22
  362.7 14.0 %collective-permute-start.19 = (f32[3,640]{1,0:T(4,128)S(1)}, f32[3,640]{1,0:T(4,128)S(1)}, u32[]{:S(2)}, u32[]{:S(2)}) collective-permute-start(f32[3,640]{1,0:T(4,128)S(1)} %get-tuple-element.44), channel_id=1, source_target_pairs={{0,64},{64,128},{128,192},{192,256},{256,320},{320,384},{384,448},... | collective-permute-start | bytes 23048 | tf_op jit(solution)/shard_map/ppermute | solution.py:15
  396.8 17.0 %scatter_fusion = f32[3,8192]{0,1:T(8,128)} fusion(f32[3,8192]{0,1:T(8,128)} %scatter_custom_fusion, s32[2560]{0:T(1024)S(1)} %reshape.430, f32[2560,3]{1,0:T(8,128)S(1)} %bitcast.327), kind=kCustom, calls=%fused_computation.16 | custom fusion | flops 7680 | bytes 102400 | tf_op jit(solution)/shard_map/scatter-add | solution.py:88
  422.7 16.9 %scatter_fusion.5 = f32[3,8192]{0,1:T(8,128)} fusion(f32[3,8192]{0,1:T(8,128)} %scatter_fusion.4, s32[2560]{0:T(1024)S(1)} %reshape.430, f32[2560,3]{1,0:T(8,128)S(1)} %bitcast.328), kind=kCustom, calls=%fused_computation.23 | custom fusion | flops 7680 | bytes 102400 | tf_op jit(solution)/shard_map/scatter-add | solution.py:88
  451.9 32.5 %gather_fusion.10 = f32[16000,3]{1,0:T(8,128)} fusion(f32[3,8192]{0,1:T(8,128)} %copy.241, s32[16384]{0:T(1024)S(1)} %pad_clamp_fusion), kind=kCustom, calls=%fused_computation.10 | custom fusion | bytes 448000 | tf_op jit(solution)/shard_map/gather | solution.py:65
  493.1 32.5 %gather_fusion.3 = f32[16000,3]{1,0:T(8,128)} fusion(f32[3,8192]{0,1:T(8,128)} %copy.208, s32[16384]{0:T(1024)S(1)} %pad_clamp_fusion), kind=kCustom, calls=%fused_computation.3 | custom fusion | bytes 448000 | tf_op jit(solution)/shard_map/gather | solution.py:65
  542.2 90.2 %scatter_custom_fusion.10 = f32[3,8192]{0,1:T(8,128)} fusion(s32[16000]{0:T(1024)} %copy-done.19, f32[16000,3]{1,0:T(8,128)} %bitcast.321, f32[]{:T(128)} %constant.13.clone.1), kind=kCustom, calls=%fused_computation.31 | custom fusion | flops 48000 | bytes 98816 | tf_op jit(solution)/shard_map/scatter-add | solution.py:67
  641.4 7.8 gather_fusion.11
  655.8 90.4 %scatter_custom_fusion.3 = f32[3,8192]{0,1:T(8,128)} fusion(s32[16000]{0:T(1024)} %copy-done.19, f32[16000,3]{1,0:T(8,128)} %bitcast.318, f32[]{:T(128)} %constant.13.clone.1), kind=kCustom, calls=%fused_computation.35 | custom fusion | flops 48000 | bytes 98816 | tf_op jit(solution)/shard_map/scatter-add | solution.py:67
  749.0 6.3 gather_fusion.4
  758.2 6.7 collective-permute-start.14
  771.4 7.9 collective-permute-start.30
  786.6 14.6 %collective-permute-start.27 = (f32[3,640]{1,0:T(4,128)S(1)}, f32[3,640]{1,0:T(4,128)S(1)}, u32[]{:S(2)}, u32[]{:S(2)}) collective-permute-start(f32[3,640]{1,0:T(4,128)S(1)} %get-tuple-element.40), channel_id=1, source_target_pairs={{0,64},{64,128},{128,192},{192,256},{256,320},{320,384},{384,448},... | collective-permute-start | bytes 23048 | tf_op jit(solution)/shard_map/ppermute | solution.py:15
  819.9 17.0 %scatter_fusion.8 = f32[3,8192]{0,1:T(8,128)} fusion(f32[3,8192]{0,1:T(8,128)} %scatter_fusion.7, s32[2560]{0:T(1024)S(1)} %reshape.430, f32[2560,3]{1,0:T(8,128)S(1)} %bitcast.329), kind=kCustom, calls=%fused_computation.27 | custom fusion | flops 7680 | bytes 102400 | tf_op jit(solution)/shard_map/scatter-add | solution.py:88
  852.1 17.0 %scatter_fusion.2 = f32[3,8192]{0,1:T(8,128)} fusion(f32[3,8192]{0,1:T(8,128)} %scatter_custom_fusion.3, s32[2560]{0:T(1024)S(1)} %reshape.430, f32[2560,3]{1,0:T(8,128)S(1)} %bitcast.326), kind=kCustom, calls=%fused_computation.19 | custom fusion | flops 7680 | bytes 102400 | tf_op jit(solution)/shard_map/scatter-add | solution.py:88
  877.6 32.5 %gather_fusion.14 = f32[16000,3]{1,0:T(8,128)} fusion(f32[3,8192]{0,1:T(8,128)} %get-tuple-element.55, s32[16384]{0:T(1024)S(1)} %pad_clamp_fusion), kind=kCustom, calls=%fused_computation.14 | custom fusion | bytes 448000 | tf_op jit(solution)/shard_map/gather | solution.py:130
  915.3 32.6 %gather_fusion.13 = f32[16000,3]{1,0:T(8,128)} fusion(f32[3,8192]{0,1:T(8,128)} %get-tuple-element.56, s32[16384]{0:T(1024)S(1)} %pad_clamp_fusion), kind=kCustom, calls=%fused_computation.13 | custom fusion | bytes 448000 | tf_op jit(solution)/shard_map/gather | solution.py:130
  (308 shorter events, 228.4 us)
Async XLA Ops:
  300.8 45.9 %collective-permute-start.5 = (f32[3,42]{1,0:T(4,128)S(1)}, f32[3,42]{1,0:T(4,128)S(1)}, u32[]{:S(2)}, u32[]{:S(2)}) collective-permute-start(f32[3,42]{1,0:T(4,128)S(1)} %bitcast.351), channel_id=1, source_target_pairs={{63,0},{64,1},{65,2},{66,3},{67,4},{68,5},{69,6},{70,7},{71,8},{72... | collective-permute-start | bytes 1520 | tf_op jit(solution)/shard_map/ppermute | solution.py:15
  305.5 50.0 %collective-permute-start.6 = (f32[3,42]{1,0:T(4,128)S(1)}, f32[3,42]{1,0:T(4,128)S(1)}, u32[]{:S(2)}, u32[]{:S(2)}) collective-permute-start(f32[3,42]{1,0:T(4,128)S(1)} %bitcast.350), channel_id=1, source_target_pairs={{0,63},{1,64},{2,65},{3,66},{4,67},{5,68},{6,69},{7,70},{8,71},{9,... | collective-permute-start | bytes 1520 | tf_op jit(solution)/shard_map/ppermute | solution.py:15
  324.3 35.8 %collective-permute-start.7 = (f32[3,42]{1,0:T(4,128)S(1)}, f32[3,42]{1,0:T(4,128)S(1)}, u32[]{:S(2)}, u32[]{:S(2)}) collective-permute-start(f32[3,42]{1,0:T(4,128)S(1)} %bitcast.348), channel_id=1, source_target_pairs={{0,65},{1,66},{2,67},{3,68},{4,69},{5,70},{6,71},{7,72},{8,73},{9,... | collective-permute-start | bytes 1520 | tf_op jit(solution)/shard_map/ppermute | solution.py:15
  325.6 35.8 %collective-permute-start.4 = (f32[3,42]{1,0:T(4,128)S(1)}, f32[3,42]{1,0:T(4,128)S(1)}, u32[]{:S(2)}, u32[]{:S(2)}) collective-permute-start(f32[3,42]{1,0:T(4,128)S(1)} %bitcast.347), channel_id=1, source_target_pairs={{65,0},{66,1},{67,2},{68,3},{69,4},{70,5},{71,6},{72,7},{73,8},{74... | collective-permute-start | bytes 1520 | tf_op jit(solution)/shard_map/ppermute | solution.py:15
  327.0 35.8 %collective-permute-start.21 = (f32[3,42]{1,0:T(4,128)S(1)}, f32[3,42]{1,0:T(4,128)S(1)}, u32[]{:S(2)}, u32[]{:S(2)}) collective-permute-start(f32[3,42]{1,0:T(4,128)S(1)} %bitcast.352), channel_id=1, source_target_pairs={{63,0},{64,1},{65,2},{66,3},{67,4},{68,5},{69,6},{70,7},{71,8},{72... | collective-permute-start | bytes 1520 | tf_op jit(solution)/shard_map/ppermute | solution.py:15
  346.7 30.1 %collective-permute-start.22 = (f32[3,42]{1,0:T(4,128)S(1)}, f32[3,42]{1,0:T(4,128)S(1)}, u32[]{:S(2)}, u32[]{:S(2)}) collective-permute-start(f32[3,42]{1,0:T(4,128)S(1)} %bitcast.360), channel_id=1, source_target_pairs={{0,63},{1,64},{2,65},{3,66},{4,67},{5,68},{6,69},{7,70},{8,71},{9,... | collective-permute-start | bytes 1520 | tf_op jit(solution)/shard_map/ppermute | solution.py:15
  355.6 23.2 %collective-permute-start.23 = (f32[3,42]{1,0:T(4,128)S(1)}, f32[3,42]{1,0:T(4,128)S(1)}, u32[]{:S(2)}, u32[]{:S(2)}) collective-permute-start(f32[3,42]{1,0:T(4,128)S(1)} %bitcast.357), channel_id=1, source_target_pairs={{0,65},{1,66},{2,67},{3,68},{4,69},{5,70},{6,71},{7,72},{8,73},{9,... | collective-permute-start | bytes 1520 | tf_op jit(solution)/shard_map/ppermute | solution.py:15
  360.1 22.9 %collective-permute-start.20 = (f32[3,42]{1,0:T(4,128)S(1)}, f32[3,42]{1,0:T(4,128)S(1)}, u32[]{:S(2)}, u32[]{:S(2)}) collective-permute-start(f32[3,42]{1,0:T(4,128)S(1)} %bitcast.354), channel_id=1, source_target_pairs={{65,0},{66,1},{67,2},{68,3},{69,4},{70,5},{71,6},{72,7},{73,8},{74... | collective-permute-start | bytes 1520 | tf_op jit(solution)/shard_map/ppermute | solution.py:15
  361.4 22.9 %collective-permute-start.16 = (f32[3,640]{1,0:T(4,128)S(1)}, f32[3,640]{1,0:T(4,128)S(1)}, u32[]{:S(2)}, u32[]{:S(2)}) collective-permute-start(f32[3,640]{1,0:T(4,128)S(1)} %get-tuple-element.43), channel_id=1, source_target_pairs={{1,0},{2,1},{3,2},{4,3},{5,4},{6,5},{7,6},{8,7},{9,8},{10,9},{11,1... | collective-permute-start | bytes 23048 | tf_op jit(solution)/shard_map/ppermute | solution.py:15
  362.7 25.5 %collective-permute-start.19 = (f32[3,640]{1,0:T(4,128)S(1)}, f32[3,640]{1,0:T(4,128)S(1)}, u32[]{:S(2)}, u32[]{:S(2)}) collective-permute-start(f32[3,640]{1,0:T(4,128)S(1)} %get-tuple-element.44), channel_id=1, source_target_pairs={{0,64},{64,128},{128,192},{192,256},{256,320},{320,384},{384,448},... | collective-permute-start | bytes 23048 | tf_op jit(solution)/shard_map/ppermute | solution.py:15
  378.8 16.8 %collective-permute-start.17 = (f32[3,640]{1,0:T(4,128)S(1)}, f32[3,640]{1,0:T(4,128)S(1)}, u32[]{:S(2)}, u32[]{:S(2)}) collective-permute-start(f32[3,640]{1,0:T(4,128)S(1)} %get-tuple-element.46), channel_id=1, source_target_pairs={{0,1},{1,2},{2,3},{3,4},{4,5},{5,6},{6,7},{7,8},{8,9},{9,10},{10,1... | collective-permute-start | bytes 23048 | tf_op jit(solution)/shard_map/ppermute | solution.py:15
  758.2 21.2 %collective-permute-start.14 = (f32[3,42]{1,0:T(4,128)S(1)}, f32[3,42]{1,0:T(4,128)S(1)}, u32[]{:S(2)}, u32[]{:S(2)}) collective-permute-start(f32[3,42]{1,0:T(4,128)S(1)} %bitcast.356), channel_id=1, source_target_pairs={{0,63},{1,64},{2,65},{3,66},{4,67},{5,68},{6,69},{7,70},{8,71},{9,... | collective-permute-start | bytes 1520 | tf_op jit(solution)/shard_map/ppermute | solution.py:15
  764.8 19.1 %collective-permute-start.15 = (f32[3,42]{1,0:T(4,128)S(1)}, f32[3,42]{1,0:T(4,128)S(1)}, u32[]{:S(2)}, u32[]{:S(2)}) collective-permute-start(f32[3,42]{1,0:T(4,128)S(1)} %bitcast.353), channel_id=1, source_target_pairs={{0,65},{1,66},{2,67},{3,68},{4,69},{5,70},{6,71},{7,72},{8,73},{9,... | collective-permute-start | bytes 1520 | tf_op jit(solution)/shard_map/ppermute | solution.py:15
  767.1 18.2 %collective-permute-start.12 = (f32[3,42]{1,0:T(4,128)S(1)}, f32[3,42]{1,0:T(4,128)S(1)}, u32[]{:S(2)}, u32[]{:S(2)}) collective-permute-start(f32[3,42]{1,0:T(4,128)S(1)} %bitcast.349), channel_id=1, source_target_pairs={{65,0},{66,1},{67,2},{68,3},{69,4},{70,5},{71,6},{72,7},{73,8},{74... | collective-permute-start | bytes 1520 | tf_op jit(solution)/shard_map/ppermute | solution.py:15
  768.4 18.2 %collective-permute-start.29 = (f32[3,42]{1,0:T(4,128)S(1)}, f32[3,42]{1,0:T(4,128)S(1)}, u32[]{:S(2)}, u32[]{:S(2)}) collective-permute-start(f32[3,42]{1,0:T(4,128)S(1)} %bitcast.346), channel_id=1, source_target_pairs={{63,0},{64,1},{65,2},{66,3},{67,4},{68,5},{69,6},{70,7},{71,8},{72... | collective-permute-start | bytes 1520 | tf_op jit(solution)/shard_map/ppermute | solution.py:15
  771.4 29.7 %collective-permute-start.30 = (f32[3,42]{1,0:T(4,128)S(1)}, f32[3,42]{1,0:T(4,128)S(1)}, u32[]{:S(2)}, u32[]{:S(2)}) collective-permute-start(f32[3,42]{1,0:T(4,128)S(1)} %bitcast.345), channel_id=1, source_target_pairs={{0,63},{1,64},{2,65},{3,66},{4,67},{5,68},{6,69},{7,70},{8,71},{9,... | collective-permute-start | bytes 1520 | tf_op jit(solution)/shard_map/ppermute | solution.py:15
  779.4 23.7 %collective-permute-start.31 = (f32[3,42]{1,0:T(4,128)S(1)}, f32[3,42]{1,0:T(4,128)S(1)}, u32[]{:S(2)}, u32[]{:S(2)}) collective-permute-start(f32[3,42]{1,0:T(4,128)S(1)} %bitcast.358), channel_id=1, source_target_pairs={{0,65},{1,66},{2,67},{3,68},{4,69},{5,70},{6,71},{7,72},{8,73},{9,... | collective-permute-start | bytes 1520 | tf_op jit(solution)/shard_map/ppermute | solution.py:15
  784.0 23.4 %collective-permute-start.28 = (f32[3,42]{1,0:T(4,128)S(1)}, f32[3,42]{1,0:T(4,128)S(1)}, u32[]{:S(2)}, u32[]{:S(2)}) collective-permute-start(f32[3,42]{1,0:T(4,128)S(1)} %bitcast.355), channel_id=1, source_target_pairs={{65,0},{66,1},{67,2},{68,3},{69,4},{70,5},{71,6},{72,7},{73,8},{74... | collective-permute-start | bytes 1520 | tf_op jit(solution)/shard_map/ppermute | solution.py:15
  785.3 23.9 %collective-permute-start.24 = (f32[3,640]{1,0:T(4,128)S(1)}, f32[3,640]{1,0:T(4,128)S(1)}, u32[]{:S(2)}, u32[]{:S(2)}) collective-permute-start(f32[3,640]{1,0:T(4,128)S(1)} %get-tuple-element.39), channel_id=1, source_target_pairs={{1,0},{2,1},{3,2},{4,3},{5,4},{6,5},{7,6},{8,7},{9,8},{10,9},{11,1... | collective-permute-start | bytes 23048 | tf_op jit(solution)/shard_map/ppermute | solution.py:15
  786.6 26.5 %collective-permute-start.27 = (f32[3,640]{1,0:T(4,128)S(1)}, f32[3,640]{1,0:T(4,128)S(1)}, u32[]{:S(2)}, u32[]{:S(2)}) collective-permute-start(f32[3,640]{1,0:T(4,128)S(1)} %get-tuple-element.40), channel_id=1, source_target_pairs={{0,64},{64,128},{128,192},{192,256},{256,320},{320,384},{384,448},... | collective-permute-start | bytes 23048 | tf_op jit(solution)/shard_map/ppermute | solution.py:15
  807.4 44.1 %collective-permute-start.8 = (f32[3,640]{1,0:T(4,128)S(1)}, f32[3,640]{1,0:T(4,128)S(1)}, u32[]{:S(2)}, u32[]{:S(2)}) collective-permute-start(f32[3,640]{1,0:T(4,128)S(1)} %get-tuple-element.47), channel_id=1, source_target_pairs={{1,0},{2,1},{3,2},{4,3},{5,4},{6,5},{7,6},{8,7},{9,8},{10,9},{11,1... | collective-permute-start | bytes 23048 | tf_op jit(solution)/shard_map/ppermute | solution.py:15
  809.1 42.4 %collective-permute-start.11 = (f32[3,640]{1,0:T(4,128)S(1)}, f32[3,640]{1,0:T(4,128)S(1)}, u32[]{:S(2)}, u32[]{:S(2)}) collective-permute-start(f32[3,640]{1,0:T(4,128)S(1)} %get-tuple-element.48), channel_id=1, source_target_pairs={{0,64},{64,128},{128,192},{192,256},{256,320},{320,384},{384,448},... | collective-permute-start | bytes 23048 | tf_op jit(solution)/shard_map/ppermute | solution.py:15
  813.1 38.5 %collective-permute-start.10 = (f32[3,640]{1,0:T(4,128)S(1)}, f32[3,640]{1,0:T(4,128)S(1)}, u32[]{:S(2)}, u32[]{:S(2)}) collective-permute-start(f32[3,640]{1,0:T(4,128)S(1)} %get-tuple-element.49), channel_id=1, source_target_pairs={{64,0},{128,64},{192,128},{256,192},{320,256},{384,320},{448,384},... | collective-permute-start | bytes 23048 | tf_op jit(solution)/shard_map/ppermute | solution.py:15
  815.0 36.5 %collective-permute-start.9 = (f32[3,640]{1,0:T(4,128)S(1)}, f32[3,640]{1,0:T(4,128)S(1)}, u32[]{:S(2)}, u32[]{:S(2)}) collective-permute-start(f32[3,640]{1,0:T(4,128)S(1)} %get-tuple-element.50), channel_id=1, source_target_pairs={{0,1},{1,2},{2,3},{3,4},{4,5},{5,6},{6,7},{7,8},{8,9},{9,10},{10,1... | collective-permute-start | bytes 23048 | tf_op jit(solution)/shard_map/ppermute | solution.py:15
  (50 other events, 2515.1 us)
where the time goes:
time: 974 us; the launch traced here: 955 us
  other arithmetic  483 us (50%)
  local copies, waits for them, and re-layouts  324 us (33%)
  starting transfers between devices  137 us (14%)
    scatter-add x4, other arithmetic, nodal_force(): nodes = jnp.zeros_like(field).at[:, connect].add(-force * keep)  361 us
    gather x8, local copies, waits for them, and re-layouts, nodal_force(): points = field[:, connect]  151 us
    ppermute x32, starting transfers between devices, shifted(): return lax.ppermute(array, axis, pairs)  137 us
    gather x4, local copies, waits for them, and re-layouts, on_device(): rho_k = rho_k + time_step * jnp.sum(accel_a[:, ibool] * points_f, 0) * keep  75.5 us
    scatter-add x4, other arithmetic, assemble(): total = force.at[:, face_list].add(jnp.stack(got_face, 1))  67.9 us
    gather x8, local copies, waits for them, and re-layouts, assemble(): face_sent = force[:, face_list] * face_keep[None]  31.2 us
    scatter-add x4, other arithmetic, assemble(): return total.at[:, edge_list].add(jnp.stack(got_edge, 1))  22.6 us
    mul x4, local copies, waits for them, and re-layouts, nodal_force(): nodes = jnp.zeros_like(field).at[:, connect].add(-force * keep)  21.6 us
  transfers between devices with their start and end apart: 32, of which 0 were waited for; matrix products, arithmetic and copies ran while one was open for 6% of the time, Pallas kernels for 0%

commit v1 on v0

v1 whole, which is shorter than its diff:
```python
import functools
import math

import jax
import jax.numpy as jnp
import ml_dtypes
import numpy as np
from jax import lax
from jax.experimental import pallas as pl
from jax.experimental.pallas import tpu as pltpu
from jax.sharding import PartitionSpec as P

time_step = 0.5
F32 = jnp.float32
BF16 = jnp.bfloat16
MESH = pl.DeviceIdType.MESH

LANES = 128
HIGH_ROWS = 32
COLUMNS = 256
FIELDS = 6
TABLE = FIELDS * HIGH_ROWS
POINT_ROWS = 128
LIST_ROWS = 24
GROUP = 8
WIDE = GROUP * LANES

face_offsets = ((0, 1), (0, -1), (1, 0), (-1, 0))
face_opposite = (1, 0, 3, 2)
edge_offsets = ((1, 1), (1, -1), (-1, 1), (-1, -1))
edge_opposite = (3, 2, 1, 0)


def gll_tables():
    points = np.array([-1.0, -math.sqrt(3.0 / 7.0), 0.0, math.sqrt(3.0 / 7.0), 1.0])
    weights = np.array([0.1, 49.0 / 90.0, 32.0 / 45.0, 49.0 / 90.0, 0.1])
    table = np.zeros((5, 5))
    for a in range(5):
        for i in range(5):
            if a != i:
                prod_a = np.prod([points[a] - points[m] for m in range(5) if m != a])
                prod_i = np.prod([points[i] - points[m] for m in range(5) if m != i])
                table[a, i] = prod_a / (prod_i * (points[a] - points[i]))
            else:
                table[a, a] = sum([1.0 / (points[a] - points[m]) for m in range(5) if m != a])
    cube = weights[:, None, None] * weights[None, :, None] * weights[None, None, :]
    return (table, cube)


def operators():
    table, cube = gll_tables()
    five = np.eye(5)
    blocks = []
    for op in (
        np.kron(np.eye(25), table),
        np.kron(np.kron(five, table), five),
        np.kron(table, np.eye(25)),
    ):
        block = np.zeros((POINT_ROWS, POINT_ROWS), np.float32)
        block[:125, :125] = op
        blocks.append(block)
    forward = np.concatenate(blocks, 0)
    backward = np.concatenate([b.T for b in blocks], 1)

    def parts(a):
        high = a.astype(ml_dtypes.bfloat16)
        low = (a - high.astype(np.float32)).astype(ml_dtypes.bfloat16)
        return jnp.asarray(np.concatenate([high, high, low], 1))

    weight = np.zeros((POINT_ROWS, LANES), np.float32)
    weight[:125] = cube.reshape(125, 1)
    return (parts(forward), parts(backward), jnp.asarray(weight))


def split(value):
    high = value.astype(BF16)
    low = (value - high.astype(F32)).astype(BF16)
    return (high, low)


def build_one_hot(index_ref, rows, hot_ref, row_ref):
    def body(i, carry):
        index = index_ref[pl.ds(pl.multiple_of(i * GROUP, GROUP), GROUP), :]
        column = jnp.bitwise_and(index, 127) + jnp.left_shift(jnp.right_shift(index, 12), 7)
        high = jnp.where(index < 0, 99, jnp.bitwise_and(jnp.right_shift(index, 7), 31))
        column = column.astype(F32).astype(BF16)
        high = high.astype(F32).astype(BF16)
        columns = lax.broadcasted_iota(jnp.int32, (COLUMNS, LANES), 0).astype(F32).astype(BF16)
        highs = lax.broadcasted_iota(jnp.int32, (HIGH_ROWS, LANES), 0).astype(F32).astype(BF16)
        one, zero = (jnp.ones((), BF16), jnp.zeros((), BF16))
        for u in range(GROUP):
            at = pl.ds(pl.multiple_of(i * WIDE + u * LANES, LANES), LANES)
            here = jnp.broadcast_to(column[u : u + 1], (COLUMNS, LANES)) == columns
            hot_ref[:, at] = jnp.where(here, one, zero)
            here = jnp.broadcast_to(high[u : u + 1], (HIGH_ROWS, LANES)) == highs
            row_ref[:, at] = jnp.where(here, one, zero)
        return carry

    lax.fori_loop(0, rows // GROUP, body, 0)


def make_table(source, fields, table_ref):
    for c in range(fields):
        high, low = split(source(c))
        at = pl.ds(c * HIGH_ROWS, HIGH_ROWS)
        for b in range(2):
            part = slice(b * HIGH_ROWS, (b + 1) * HIGH_ROWS)
            table_ref[at, b * LANES : (b + 1) * LANES] = high[part]
            table_ref[at, COLUMNS + b * LANES : COLUMNS + (b + 1) * LANES] = low[part]


def gather(table_ref, fields, rows, hot_ref, row_ref, put):
    height = fields * HIGH_ROWS

    def body(i, carry):
        at = pl.ds(pl.multiple_of(i * WIDE, WIDE), WIDE)
        hot = hot_ref[:, at]
        found = jnp.dot(table_ref[:height, :COLUMNS], hot, preferred_element_type=F32)
        found += jnp.dot(table_ref[:height, COLUMNS:], hot, preferred_element_type=F32)
        mask = row_ref[:, at].astype(F32)
        for c in range(fields):
            part = found[c * HIGH_ROWS : (c + 1) * HIGH_ROWS]
            value = jnp.sum(part * mask, axis=0, keepdims=True)
            for u in range(GROUP):
                put(i, u, c, value[:, u * LANES : (u + 1) * LANES])
        return carry

    lax.fori_loop(0, rows // GROUP, body, 0)


def scatter(load, rows, hot_ref, row_ref, masked_ref, total_ref):
    def body(i, carry):
        at = pl.ds(pl.multiple_of(i * WIDE, WIDE), WIDE)
        group = load(i)
        for u in range(GROUP):
            mask = row_ref[:, pl.ds(pl.multiple_of(i * WIDE + u * LANES, LANES), LANES)]
            values = group(u)
            lanes = slice(u * LANES, (u + 1) * LANES)
            for c in range(FIELDS):
                high, low = split(values[c])
                top = c * HIGH_ROWS
                masked_ref[top : top + HIGH_ROWS, lanes] = mask * jnp.broadcast_to(
                    high, (HIGH_ROWS, LANES)
                )
                top = TABLE + c * HIGH_ROWS
                masked_ref[top : top + HIGH_ROWS, lanes] = mask * jnp.broadcast_to(
                    low, (HIGH_ROWS, LANES)
                )
        added = lax.dot_general(
            masked_ref[...],
            hot_ref[:, at],
            (((1,), (1,)), ((), ())),
            preferred_element_type=F32,
        )
        total_ref[...] += added[:TABLE] + added[TABLE:]
        return carry

    lax.fori_loop(0, rows // GROUP, body, 0)


def element_force(
    points_ref, bulk_ref, shear_ref, weight_ref, jac_ref, keep, forward_op, backward_op,
    rhs_ref, grad_ref, flux_ref, force_ref, kappa_ref, mu_ref, first,
):
    for c in range(FIELDS):
        high, low = split(points_ref[c])
        lanes = slice(c * LANES, (c + 1) * LANES)
        rhs_ref[0:128, lanes] = high
        rhs_ref[128:256, lanes] = low
        rhs_ref[256:384, lanes] = high
    grad_ref[...] = jnp.dot(forward_op[...], rhs_ref[...], preferred_element_type=F32)
    scales = [jac_ref[d : d + 1, :] for d in range(3)]
    inverse = -keep / (scales[0] * scales[1] * scales[2])

    def body(i, carry):
        tile = 16
        at = pl.ds(pl.multiple_of(i * tile, tile), tile)
        bulk, shear = (bulk_ref[at, :], shear_ref[at, :])
        weight = weight_ref[at, :] * inverse
        divs, devs = ([], [])
        for f in range(2):
            grads = [
                [
                    grad_ref[
                        pl.ds(pl.multiple_of(d * 128 + i * tile, tile), tile),
                        (f * 3 + c) * LANES : (f * 3 + c + 1) * LANES,
                    ]
                    * scales[d]
                    for d in range(3)
                ]
                for c in range(3)
            ]
            div = grads[0][0] + grads[1][1] + grads[2][2]
            lame = (bulk - 2.0 / 3.0 * shear) * div
            third = div / 3.0
            strain = {}
            for c in range(3):
                for d in range(c, 3):
                    strain[c, d] = 0.5 * (grads[c][d] + grads[d][c]) if c != d else grads[c][c]
            for c in range(3):
                for d in range(3):
                    stress = 2.0 * shear * strain[min(c, d), max(c, d)]
                    if c == d:
                        stress = stress + lame
                    high, low = split(stress * weight * scales[d])
                    lanes = slice((f * 3 + c) * LANES, (f * 3 + c + 1) * LANES)
                    for part, value in ((0, high), (1, low), (2, high)):
                        top = pl.multiple_of(part * 384 + d * 128 + i * tile, tile)
                        flux_ref[pl.ds(top, tile), lanes] = value
            divs.append(div)
            devs.append(
                {key: value - third if key[0] == key[1] else value for key, value in strain.items()}
            )
        both = 0.0
        for c in range(3):
            for d in range(c, 3):
                term = devs[0][c, d] * devs[1][c, d]
                both = both + (term if c == d else 2.0 * term)
        kappa_add = time_step * divs[0] * divs[1] * keep
        mu_add = 2.0 * time_step * both * keep
        if first:
            kappa_ref[at, :] = kappa_add
            mu_ref[at, :] = mu_add
        else:
            kappa_ref[at, :] += kappa_add
            mu_ref[at, :] += mu_add
        return carry

    lax.fori_loop(0, POINT_ROWS // 16, body, 0)
    force_ref[...] = jnp.dot(backward_op[...], flux_ref[...], preferred_element_type=F32)


def partners():
    row, col = (lax.axis_index("row"), lax.axis_index("col"))
    rows, cols = (lax.axis_size("row"), lax.axis_size("col"))

    def at(offset):
        return (
            lax.rem(row + offset[0] + rows, rows),
            lax.rem(col + offset[1] + cols, cols),
        )

    messages = []
    for s in range(4):
        messages.append((pl.ds(s * 6, 5), pl.ds(face_opposite[s] * 6, 5), at(face_offsets[s])))
    for s in range(4):
        messages.append(
            (pl.ds(s * 6 + 5, 1), pl.ds(edge_opposite[s] * 6 + 5, 1), at(edge_offsets[s]))
        )
    return messages


def kernel(
    steps, count_ref, face_len_ref, edge_len_ref,
    fwd_ref, fwd_prev_ref, adj_ref, adj_prev_ref, mass_ref, ibool_ref, jac_ref, kap_ref, mod_ref,
    face_ref, edge_ref, rec_ref, src_ref, forward_op, backward_op, weight_ref,
    fwd_out, adj_out, rho_out, kappa_out, mu_out,
    now, prev, density, index, list_index, hot, row_hot, list_hot, list_row, table, points,
    bulk, shear, rhs, grad, flux, force, masked, total, kappa_sum, mu_sum, send, recv,
    send_sem, recv_sem,
):
    messages = partners()
    barrier = pltpu.get_barrier_semaphore()
    for _, _, device in messages:
        pl.semaphore_signal(barrier, inc=1, device_id=device, device_id_type=MESH)

    lane = lax.broadcasted_iota(jnp.int32, (1, LANES), 1)
    keep = jnp.where(lane < count_ref[0], 1.0, 0.0).astype(F32)

    index[...] = jnp.full((POINT_ROWS, LANES), -1, jnp.int32)
    index[0:125, :] = ibool_ref[...]
    bulk[...] = jnp.zeros((POINT_ROWS, LANES), F32)
    bulk[0:125, :] = kap_ref[...]
    shear[...] = jnp.zeros((POINT_ROWS, LANES), F32)
    shear[0:125, :] = mod_ref[...]
    list_index[...] = jnp.full((LIST_ROWS, LANES), -1, jnp.int32)
    width = edge_ref.shape[2]
    narrow = lax.broadcasted_iota(jnp.int32, (1, width), 1)
    for s in range(4):
        for k in range(5):
            nodes = face_ref[0, s : s + 1, k * LANES : (k + 1) * LANES]
            live = lane + k * LANES < face_len_ref[0, s]
            list_index[s * 6 + k : s * 6 + k + 1, :] = jnp.where(live, nodes, -1)
        nodes = edge_ref[0, s : s + 1, :]
        live = narrow < edge_len_ref[0, s]
        list_index[s * 6 + 5 : s * 6 + 6, 0:width] = jnp.where(live, nodes, -1)

    def spread(r, carry):
        at = pl.ds(pl.multiple_of(r * LANES, LANES), LANES)
        for base, target, source in (
            (0, now, fwd_ref), (3, now, adj_ref), (0, prev, fwd_prev_ref), (3, prev, adj_prev_ref),
        ):
            value = source[:, at]
            for c in range(3):
                target[base + c, pl.ds(r, 1), :] = value[c : c + 1]
        return carry

    lax.fori_loop(0, 64, spread, 0)
    density[...] = jnp.zeros((64, LANES), F32)
    send[...] = jnp.zeros(send.shape, F32)

    build_one_hot(index, POINT_ROWS, hot, row_hot)
    build_one_hot(list_index, LIST_ROWS, list_hot, list_row)

    element = lax.broadcasted_iota(jnp.int32, (LANES, LANES), 0)
    chosen = jnp.where(
        jnp.broadcast_to(rec_ref[...], (LANES, LANES)) == element, 1.0, 0.0
    ).astype(BF16)

    for step in range(steps):
        make_table(lambda c: now[c], FIELDS, table)

        def put_point(i, u, c, value):
            at = pl.multiple_of(i * GROUP, GROUP) + u
            points[c, pl.ds(at, 1), :] = value

        gather(table, FIELDS, POINT_ROWS, hot, row_hot, put_point)
        element_force(
            points, bulk, shear, weight_ref, jac_ref, keep, forward_op, backward_op,
            rhs, grad, flux, force, kappa_sum, mu_sum, step == 0,
        )
        for c in range(3):
            high, low = split(src_ref[step, c : c + 1, :])
            rest = (src_ref[step, c : c + 1, :] - high.astype(F32) - low.astype(F32)).astype(BF16)
            stack = jnp.concatenate(
                [jnp.broadcast_to(part.astype(F32), (8, LANES)) for part in (high, low, rest)], 0
            ).astype(BF16)
            found = lax.dot_general(
                stack, chosen, (((1,), (1,)), ((), ())), preferred_element_type=F32
            )
            lanes = slice((3 + c) * LANES, (4 + c) * LANES)
            force[62:63, lanes] += found[0:1] + found[8:9] + found[16:17]

        total[...] = jnp.zeros((TABLE, COLUMNS), F32)

        def load_point(i):
            block = force[pl.ds(pl.multiple_of(i * GROUP, GROUP), GROUP), :]
            return lambda u: [block[u : u + 1, c * LANES : (c + 1) * LANES] for c in range(FIELDS)]

        scatter(load_point, POINT_ROWS, hot, row_hot, masked, total)

        high, low = split(total[...])
        table[:, :COLUMNS] = high
        table[:, COLUMNS:] = low

        def put_list(i, u, c, value):
            send[step, i * GROUP + u, c : c + 1, :] = value

        gather(table, FIELDS, LIST_ROWS, list_hot, list_row, put_list)

        if step == 0:
            pl.semaphore_wait(barrier, len(messages))
        copies = []
        for slot, (source, target, device) in enumerate(messages):
            landing = face_opposite[slot] if slot < 4 else 4 + edge_opposite[slot - 4]
            copy = pltpu.make_async_remote_copy(
                src_ref=send.at[step, source],
                dst_ref=recv.at[step, target],
                send_sem=send_sem.at[step, slot],
                recv_sem=recv_sem.at[step, landing],
                device_id=device,
                device_id_type=MESH,
            )
            copy.start()
            copies.append(copy)
        for copy in copies:
            copy.wait()

        def load_list(i):
            return lambda u: [recv[step, i * GROUP + u, c : c + 1, :] for c in range(FIELDS)]

        scatter(load_list, LIST_ROWS, list_hot, list_row, masked, total)

        for b in range(2):
            part = pl.ds(b * HIGH_ROWS, HIGH_ROWS)
            lanes = slice(b * LANES, (b + 1) * LANES)
            mass = mass_ref[part, :]
            accel = [
                mass * total[c * HIGH_ROWS : (c + 1) * HIGH_ROWS, lanes] for c in range(FIELDS)
            ]
            both = 0.0
            for c in range(3):
                both = both + accel[3 + c] * now[c, part, :]
            density[part, :] += time_step * both
            for c in range(FIELDS):
                field = now[c, part, :]
                later = 2.0 * field - prev[c, part, :] + time_step * time_step * accel[c]
                prev[c, part, :] = field
                now[c, part, :] = later

    def join(r, carry):
        at = pl.ds(pl.multiple_of(r * LANES, LANES), LANES)
        for base, target in ((0, fwd_out), (3, adj_out)):
            for c in range(3):
                target[c : c + 1, at] = now[base + c, pl.ds(r, 1), :]
        return carry

    lax.fori_loop(0, 64, join, 0)
    make_table(lambda c: density[...], 1, table)

    def put_density(i, u, c, value):
        at = pl.multiple_of(i * GROUP, GROUP) + u
        points[0, pl.ds(at, 1), :] = value

    gather(table, 1, POINT_ROWS, hot, row_hot, put_density)
    rho_out[...] = points[0, 0:125, :] * keep
    kappa_out[...] = kappa_sum[0:125, :]
    mu_out[...] = mu_sum[0:125, :]


def on_device(
    fwd_now, fwd_prev, adj_now, adj_prev, inv_mass, ibool, inv_jac, kappa, mu, elem_count,
    face_nodes, face_len, edge_nodes, edge_len, rec_elem, adj_src,
):
    forward_op, backward_op, weight = operators()
    steps = adj_src.shape[0]
    nodes = fwd_now.shape[1]
    elements = ibool.shape[1]
    vmem = pl.BlockSpec(memory_space=pltpu.VMEM)
    smem = pl.BlockSpec(memory_space=pltpu.SMEM)
    spread = POINT_ROWS * LANES
    listed = LIST_ROWS * LANES
    scratch = [
        pltpu.VMEM((FIELDS, 64, LANES), F32),
        pltpu.VMEM((FIELDS, 64, LANES), F32),
        pltpu.VMEM((64, LANES), F32),
        pltpu.VMEM((POINT_ROWS, LANES), jnp.int32),
        pltpu.VMEM((LIST_ROWS, LANES), jnp.int32),
        pltpu.VMEM((COLUMNS, spread), BF16),
        pltpu.VMEM((HIGH_ROWS, spread), BF16),
        pltpu.VMEM((COLUMNS, listed), BF16),
        pltpu.VMEM((HIGH_ROWS, listed), BF16),
        pltpu.VMEM((TABLE, 2 * COLUMNS), BF16),
        pltpu.VMEM((FIELDS, POINT_ROWS, LANES), F32),
        pltpu.VMEM((POINT_ROWS, LANES), F32),
        pltpu.VMEM((POINT_ROWS, LANES), F32),
        pltpu.VMEM((384, FIELDS * LANES), BF16),
        pltpu.VMEM((384, FIELDS * LANES), F32),
        pltpu.VMEM((3 * 384, FIELDS * LANES), BF16),
        pltpu.VMEM((POINT_ROWS, FIELDS * LANES), F32),
        pltpu.VMEM((2 * TABLE, WIDE), BF16),
        pltpu.VMEM((TABLE, COLUMNS), F32),
        pltpu.VMEM((POINT_ROWS, LANES), F32),
        pltpu.VMEM((POINT_ROWS, LANES), F32),
        pltpu.VMEM((steps, LIST_ROWS, 8, LANES), F32),
        pltpu.VMEM((steps, LIST_ROWS, 8, LANES), F32),
        pltpu.SemaphoreType.DMA((steps, 8)),
        pltpu.SemaphoreType.DMA((steps, 8)),
    ]
    point = jax.ShapeDtypeStruct((125, elements), F32)
    node = jax.ShapeDtypeStruct((3, nodes), F32)
    return pl.pallas_call(
        functools.partial(kernel, steps),
        out_shape=(node, node, point, point, point),
        in_specs=[smem] * 3 + [vmem] * 16,
        out_specs=(vmem,) * 5,
        scratch_shapes=scratch,
        compiler_params=pltpu.CompilerParams(
            collective_id=0, has_side_effects=True, vmem_limit_bytes=40 << 20
        ),
    )(
        elem_count, face_len, edge_len,
        fwd_now, fwd_prev, adj_now, adj_prev, inv_mass.reshape(64, LANES), ibool, inv_jac, kappa, mu,
        face_nodes, edge_nodes, rec_elem.reshape(1, elements), adj_src,
        forward_op, backward_op, weight,
    )


def solution(mesh):
    field = P(None, ("row", "col"))
    part = P(("row", "col"))
    in_specs = (
        field, field, field, field, part, field, field, field, field, part,
        P(("row", "col"), None, None), P(("row", "col"), None),
        P(("row", "col"), None, None), P(("row", "col"), None),
        part, P(None, None, ("row", "col")),
    )
    return jax.shard_map(
        on_device, mesh=mesh, in_specs=in_specs, out_specs=(field,) * 5, check_vma=False
    )
```

time: 974 us -> 89.5 us (0.09); the launches traced: 955 us -> 88.8 us
  other arithmetic: 483 us -> 0 us
  local copies, waits for them, and re-layouts: 324 us -> 15.5 us
  starting transfers between devices: 137 us -> 0 us
  Pallas kernels: 0 us -> 71.9 us
    scatter-add x14 -> x0, other arithmetic: 463 us -> none  [the longest x4 361 us: nodal_force(): nodes = jnp.zeros_like(field).at[:, connect].add(-force * keep)]
    gather x33 -> x0, local copies, waits for them, and re-layouts: 271 us -> none  [the longest x8 151 us: nodal_force(): points = field[:, connect]]
    ppermute x32 -> x0, starting transfers between devices: 137 us -> none  [shifted(): return lax.ppermute(array, axis, pairs)]
    pallas_call x0 -> x1, Pallas kernels: none -> 71.9 us  [on_device(): pl.pallas_call(functools.partial(kernel, steps), out_shape=(node, node, p...]
    mul x4 -> x0, local copies, waits for them, and re-layouts: 21.6 us -> none  [nodal_force(): nodes = jnp.zeros_like(field).at[:, connect].add(-force * keep)]
    scatter-add x4 -> x0, local copies, waits for them, and re-layouts: 11.4 us -> none  [assemble(): return total.at[:, edge_list].add(jnp.stack(got_edge, 1))]
  transfers between devices with their start and end apart: 32 -> 0, of which waited for: 0 -> 0; matrix products, arithmetic and copies ran while one was open for 6% -> 0% of each run, Pallas kernels for 0% -> 0%
where the time goes in v1:
time: 89.5 us; the launch traced here: 88.8 us
  Pallas kernels  71.9 us (80%)
  local copies, waits for them, and re-layouts  15.5 us (17%)
  between operations  1.35 us (2%)
    pallas_call x1, Pallas kernels, on_device(): pl.pallas_call(functools.partial(kernel, steps), out_shape=(node, node, p...  71.9 us
    unnamed x40, local copies, waits for them, and re-layouts  15.5 us

profile of v1, /device:TPU:1, one launch (start us, length us, event | category | flops | bytes accessed | tf_op | source)
XLA Modules:
  0.0 88.8 jit_solution(7331547121040745200)
XLA Ops:
  1.3 0.0 copy-start.12
  1.3 0.0 copy-start.14
  1.3 0.7 copy.24.src_ref
  2.0 0.0 copy-start
  2.0 1.0 %copy-done = bf16[128,1152]{1,0:T(8,128)(2,1)S(1)} copy-done((bf16[128,1152]{1,0:T(8,128)(2,1)S(1)}, bf16[128,1152]{1,0:T(8,128)(2,1)}, u32[]{:S(2)}) %copy-start) | copy-done | bytes 294936
  3.0 1.0 %copy-done.1 = bf16[384,384]{1,0:T(8,128)(2,1)S(1)} copy-done((bf16[384,384]{1,0:T(8,128)(2,1)S(1)}, bf16[384,384]{1,0:T(8,128)(2,1)}, u32[]{:S(2)}) %copy-start.1) | copy-done | bytes 294936
  4.0 0.9 %copy-done.2 = f32[3,8192]{1,0:T(4,128)S(1)} copy-done((f32[3,8192]{1,0:T(4,128)S(1)}, f32[3,8192]{1,0:T(4,128)}, u32[]{:S(2)}) %copy-start.2) | copy-done | bytes 98328
  4.9 0.9 %copy-done.3 = f32[3,8192]{1,0:T(4,128)S(1)} copy-done((f32[3,8192]{1,0:T(4,128)S(1)}, f32[3,8192]{1,0:T(4,128)}, u32[]{:S(2)}) %copy-start.3) | copy-done | bytes 98328
  5.8 0.9 %copy-done.4 = f32[3,8192]{1,0:T(4,128)S(1)} copy-done((f32[3,8192]{1,0:T(4,128)S(1)}, f32[3,8192]{1,0:T(4,128)}, u32[]{:S(2)}) %copy-start.4) | copy-done | bytes 98328
  6.7 0.9 %copy-done.5 = f32[3,8192]{1,0:T(4,128)S(1)} copy-done((f32[3,8192]{1,0:T(4,128)S(1)}, f32[3,8192]{1,0:T(4,128)}, u32[]{:S(2)}) %copy-start.5) | copy-done | bytes 98328
  7.6 0.8 copy-done.6
  8.4 0.8 copy-done.7
  9.3 0.8 copy-done.8
  10.1 0.8 copy-done.9
  10.9 0.8 copy-done.10
  11.7 0.7 copy-done.13
  12.4 0.7 copy-done.15
  13.0 0.7 copy-done.16
  13.7 71.9 %shard_map.218 = (f32[3,8192]{1,0:T(4,128)S(1)}, f32[3,8192]{1,0:T(4,128)S(1)}, f32[125,128]{1,0:T(8,128)S(1)}, f32[125,128]{1,0:T(8,128)S(1)}, f32[125,128]{1,0:T(8,128)S(1)}) custom-call(s32[1]{0:T(128)S(6)} %copy.30.count_ref, s32[1,4]{1,0:T(1,128)S(1)} %copy-done.14, s32[1,4]{1,0:T(1,128)S(1)} %copy-done.15, f32[3,8192]{1,0:T(4,128)S(1)} %copy-done.2, ...), custom_call_target="tpu_custom_call" | custom-call | tf_op jit(solution)/shard_map/pallas_call | solution.py:452
  85.6 0.7 copy.31
  86.3 0.7 copy.32
  86.9 0.6 copy.33
  87.6 0.6 copy.34
  88.2 0.6 copy.35
  (17 shorter events, 0.0 us)
Async XLA Ops:
  0.6 1.4 %copy-start.11 = (s32[1,4,640]{2,1,0:T(4,128)S(1)}, s32[1,4,640]{2,1,0:T(4,128)}, u32[]{:S(2)}) copy-start(s32[1,4,640]{2,1,0:T(4,128)} %face_ref.1) | copy-start | bytes 30724
  1.3 0.7 copy-start.12
  1.3 0.7 copy-start.14
  2.0 1.0 %copy-start = (bf16[128,1152]{1,0:T(8,128)(2,1)S(1)}, bf16[128,1152]{1,0:T(8,128)(2,1)}, u32[]{:S(2)}) copy-start(bf16[128,1152]{1,0:T(8,128)(2,1)} %constant.7.clone.backward_op) | copy-start | bytes 884740
  3.0 1.0 %copy-start.1 = (bf16[384,384]{1,0:T(8,128)(2,1)S(1)}, bf16[384,384]{1,0:T(8,128)(2,1)}, u32[]{:S(2)}) copy-start(bf16[384,384]{1,0:T(8,128)(2,1)} %constant.6.clone.forward_op) | copy-start | bytes 884740
  4.0 0.9 %copy-start.2 = (f32[3,8192]{1,0:T(4,128)S(1)}, f32[3,8192]{1,0:T(4,128)}, u32[]{:S(2)}) copy-start(f32[3,8192]{1,0:T(4,128)} %fwd_ref.1) | copy-start | bytes 294916
  4.9 0.9 %copy-start.3 = (f32[3,8192]{1,0:T(4,128)S(1)}, f32[3,8192]{1,0:T(4,128)}, u32[]{:S(2)}) copy-start(f32[3,8192]{1,0:T(4,128)} %fwd_prev_ref.1) | copy-start | bytes 294916
  5.8 0.9 %copy-start.4 = (f32[3,8192]{1,0:T(4,128)S(1)}, f32[3,8192]{1,0:T(4,128)}, u32[]{:S(2)}) copy-start(f32[3,8192]{1,0:T(4,128)} %adj_ref.1) | copy-start | bytes 294916
  6.7 0.9 %copy-start.5 = (f32[3,8192]{1,0:T(4,128)S(1)}, f32[3,8192]{1,0:T(4,128)}, u32[]{:S(2)}) copy-start(f32[3,8192]{1,0:T(4,128)} %adj_prev_ref.1) | copy-start | bytes 294916
  7.6 0.8 copy-start.6
  8.4 0.8 copy-start.7
  9.3 0.8 copy-start.8
  10.1 0.8 copy-start.9
  10.9 0.8 copy-start.10
  11.7 0.7 copy-start.13
  12.4 0.7 copy-start.15
  13.0 0.7 copy-start.16

commit v2 on v1

v2 whole, which is shorter than its diff:
```python
import functools
import math

import jax
import jax.numpy as jnp
import ml_dtypes
import numpy as np
from jax import lax
from jax.experimental import pallas as pl
from jax.experimental.pallas import tpu as pltpu
from jax.sharding import PartitionSpec as P

time_step = 0.5
F32 = jnp.float32
BF16 = jnp.bfloat16
MESH = pl.DeviceIdType.MESH

LANES = 128
HIGH_ROWS = 32
COLUMNS = 256
FIELDS = 6
TABLE = FIELDS * HIGH_ROWS
POINT_ROWS = 128
LIST_ROWS = 24
GROUP = 8
WIDE = GROUP * LANES
GATHER_ROWS = 64
SCATTER_ROWS = 64

face_offsets = ((0, 1), (0, -1), (1, 0), (-1, 0))
face_opposite = (1, 0, 3, 2)
edge_offsets = ((1, 1), (1, -1), (-1, 1), (-1, -1))
edge_opposite = (3, 2, 1, 0)


def gll_tables():
    points = np.array([-1.0, -math.sqrt(3.0 / 7.0), 0.0, math.sqrt(3.0 / 7.0), 1.0])
    weights = np.array([0.1, 49.0 / 90.0, 32.0 / 45.0, 49.0 / 90.0, 0.1])
    table = np.zeros((5, 5))
    for a in range(5):
        for i in range(5):
            if a != i:
                prod_a = np.prod([points[a] - points[m] for m in range(5) if m != a])
                prod_i = np.prod([points[i] - points[m] for m in range(5) if m != i])
                table[a, i] = prod_a / (prod_i * (points[a] - points[i]))
            else:
                table[a, a] = sum([1.0 / (points[a] - points[m]) for m in range(5) if m != a])
    cube = weights[:, None, None] * weights[None, :, None] * weights[None, None, :]
    return (table, cube)


def operators():
    table, cube = gll_tables()
    five = np.eye(5)
    blocks = []
    for op in (
        np.kron(np.eye(25), table),
        np.kron(np.kron(five, table), five),
        np.kron(table, np.eye(25)),
    ):
        block = np.zeros((POINT_ROWS, POINT_ROWS), np.float32)
        block[:125, :125] = op
        blocks.append(block)
    forward = np.concatenate(blocks, 0)
    backward = np.concatenate([b.T for b in blocks], 1)

    def parts(a):
        high = a.astype(ml_dtypes.bfloat16)
        low = (a - high.astype(np.float32)).astype(ml_dtypes.bfloat16)
        return jnp.asarray(np.concatenate([high, high, low], 1))

    weight = np.zeros((POINT_ROWS, LANES), np.float32)
    weight[:125] = cube.reshape(125, 1)
    return (parts(forward), parts(backward), jnp.asarray(weight))


def split(value):
    high = value.astype(BF16)
    low = (value - high.astype(F32)).astype(BF16)
    return (high, low)


def build_one_hot(index_ref, rows, hot_ref, row_ref):
    def body(i, carry):
        index = index_ref[pl.ds(pl.multiple_of(i * GROUP, GROUP), GROUP), :]
        column = jnp.bitwise_and(index, 127) + jnp.left_shift(jnp.right_shift(index, 12), 7)
        high = jnp.where(index < 0, 99, jnp.bitwise_and(jnp.right_shift(index, 7), 31))
        column = column.astype(F32).astype(BF16)
        high = high.astype(F32).astype(BF16)
        columns = lax.broadcasted_iota(jnp.int32, (COLUMNS, LANES), 0).astype(F32).astype(BF16)
        highs = lax.broadcasted_iota(jnp.int32, (HIGH_ROWS, LANES), 0).astype(F32).astype(BF16)
        one, zero = (jnp.ones((), BF16), jnp.zeros((), BF16))
        for u in range(GROUP):
            at = pl.ds(pl.multiple_of(i * WIDE + u * LANES, LANES), LANES)
            here = jnp.broadcast_to(column[u : u + 1], (COLUMNS, LANES)) == columns
            hot_ref[:, at] = jnp.where(here, one, zero)
            here = jnp.broadcast_to(high[u : u + 1], (HIGH_ROWS, LANES)) == highs
            row_ref[:, at] = jnp.where(here, one, zero)
        return carry

    lax.fori_loop(0, rows // GROUP, body, 0)


def make_table(source, fields, table_ref):
    for c in range(fields):
        for k, value in enumerate(split(source(c))):
            at = pl.ds((k * fields + c) * HIGH_ROWS, HIGH_ROWS)
            for b in range(2):
                part = slice(b * HIGH_ROWS, (b + 1) * HIGH_ROWS)
                table_ref[at, b * LANES : (b + 1) * LANES] = value[part]


def sum_rows(parts):
    row = lax.broadcasted_iota(jnp.int32, (GROUP, LANES), 0)

    def merge(first, second, bit):
        own = jnp.bitwise_and(row, bit) == 0
        return jnp.where(own, first, second) + pltpu.roll(jnp.where(own, second, first), bit, 0)

    parts = [merge(parts[u], parts[u + 1], 1) for u in range(0, 8, 2)]
    parts = [merge(parts[0], parts[1], 2), merge(parts[2], parts[3], 2)]
    return merge(parts[0], parts[1], 4)


def gather(table_ref, fields, rows, chunk, hot_ref, row_ref, put):
    height = fields * HIGH_ROWS

    def body(j, carry):
        start = pl.multiple_of(j * chunk * LANES, LANES)
        found = jnp.dot(
            table_ref[: 2 * height, :],
            hot_ref[:, pl.ds(start, chunk * LANES)],
            preferred_element_type=F32,
        )
        for g in range(chunk // GROUP):
            sums = [[] for c in range(fields)]
            for u in range(GROUP):
                at = (g * GROUP + u) * LANES
                lanes = slice(at, at + LANES)
                mask = row_ref[:, pl.ds(pl.multiple_of(start + at, LANES), LANES)].astype(F32)
                for c in range(fields):
                    top = c * HIGH_ROWS
                    part = found[top : top + HIGH_ROWS, lanes]
                    part = part + found[height + top : height + top + HIGH_ROWS, lanes]
                    part = part * mask
                    sums[c].append((part[0:8] + part[8:16]) + (part[16:24] + part[24:32]))
            for c in range(fields):
                put(j * (chunk // GROUP) + g, c, sum_rows(sums[c]))
        return carry

    if rows == chunk:
        body(0, 0)
    else:
        lax.fori_loop(0, rows // chunk, body, 0)


def scatter(load, rows, chunk, hot_ref, row_ref, masked_ref, total_ref):
    def body(j, carry):
        start = pl.multiple_of(j * chunk * LANES, LANES)

        def fill(i, carry):
            group = load(j * (chunk // GROUP) + i)
            for u in range(GROUP):
                at = pl.multiple_of(i * WIDE + u * LANES, LANES)
                mask = row_ref[:, pl.ds(pl.multiple_of(start + at, LANES), LANES)]
                for c in range(FIELDS):
                    for k, value in enumerate(group(u, c)):
                        top = k * TABLE + c * HIGH_ROWS
                        masked_ref[top : top + HIGH_ROWS, pl.ds(at, LANES)] = (
                            mask * jnp.broadcast_to(value, (HIGH_ROWS, LANES))
                        )
            return carry

        lax.fori_loop(0, chunk // GROUP, fill, 0, unroll=True)
        found = lax.dot_general(
            masked_ref[:, : chunk * LANES],
            hot_ref[:, pl.ds(start, chunk * LANES)],
            (((1,), (1,)), ((), ())),
            preferred_element_type=F32,
        )
        total_ref[...] += found[:TABLE] + found[TABLE:]
        return carry

    if rows == chunk:
        body(0, 0)
    else:
        lax.fori_loop(0, rows // chunk, body, 0)


def strains(grad_ref, scales, i, tile, f):
    grads = [
        [
            grad_ref[
                pl.ds(pl.multiple_of(d * POINT_ROWS + i * tile, tile), tile),
                (f * 3 + c) * LANES : (f * 3 + c + 1) * LANES,
            ]
            * scales[d]
            for d in range(3)
        ]
        for c in range(3)
    ]
    strain = {}
    for c in range(3):
        for d in range(c, 3):
            strain[c, d] = 0.5 * (grads[c][d] + grads[d][c]) if c != d else grads[c][c]
    return (strain[0, 0] + strain[1, 1] + strain[2, 2], strain)


def element_force(
    points_ref, bulk_ref, shear_ref, weight_ref, scales, keep, forward_op, backward_op,
    rhs_ref, grad_ref, flux_ref, force_ref,
):
    for c in range(FIELDS):
        high, low = split(points_ref[c])
        lanes = slice(c * LANES, (c + 1) * LANES)
        rhs_ref[0:128, lanes] = high
        rhs_ref[128:256, lanes] = low
        rhs_ref[256:384, lanes] = high
    grad_ref[...] = jnp.dot(forward_op[...], rhs_ref[...], preferred_element_type=F32)
    inverse = -keep / (scales[0] * scales[1] * scales[2])

    def body(i, carry):
        tile = 16
        at = pl.ds(pl.multiple_of(i * tile, tile), tile)
        weight = weight_ref[at, :] * inverse
        double = 2.0 * shear_ref[at, :] * weight
        lame = (bulk_ref[at, :] - 2.0 / 3.0 * shear_ref[at, :]) * weight
        for f in range(2):
            div, strain = strains(grad_ref, scales, i, tile, f)
            for c in range(3):
                for d in range(c, 3):
                    stress = double * strain[c, d]
                    if c == d:
                        stress = stress + lame * div
                    for e, g in ((c, d), (d, c))[: 1 + (c != d)]:
                        high, low = split(stress * scales[g])
                        lanes = slice((f * 3 + e) * LANES, (f * 3 + e + 1) * LANES)
                        for part, value in ((0, high), (1, low), (2, high)):
                            top = pl.multiple_of(part * 384 + g * POINT_ROWS + i * tile, tile)
                            flux_ref[pl.ds(top, tile), lanes] = value
        return carry

    lax.fori_loop(0, POINT_ROWS // 16, body, 0, unroll=4)
    force_ref[...] = jnp.dot(backward_op[...], flux_ref[...], preferred_element_type=F32)


def add_moduli_kernels(grad_ref, scales, keep, kappa_ref, mu_ref):
    def body(i, carry):
        tile = 16
        at = pl.ds(pl.multiple_of(i * tile, tile), tile)
        divs, devs = ([], [])
        for f in range(2):
            div, strain = strains(grad_ref, scales, i, tile, f)
            third = div / 3.0
            divs.append(div)
            devs.append({k: v - third if k[0] == k[1] else v for k, v in strain.items()})
        even = sum(devs[0][c, c] * devs[1][c, c] for c in range(3))
        odd = sum(devs[0][key] * devs[1][key] for key in ((0, 1), (0, 2), (1, 2)))
        kappa_ref[at, :] += time_step * divs[0] * divs[1] * keep
        mu_ref[at, :] += 2.0 * time_step * (even + 2.0 * odd) * keep
        return carry

    lax.fori_loop(0, POINT_ROWS // 16, body, 0, unroll=4)


def partners():
    row, col = (lax.axis_index("row"), lax.axis_index("col"))
    rows, cols = (lax.axis_size("row"), lax.axis_size("col"))

    def at(offset):
        return (
            lax.rem(row + offset[0] + rows, rows),
            lax.rem(col + offset[1] + cols, cols),
        )

    messages = []
    for s in range(4):
        messages.append((pl.ds(s * 6, 5), pl.ds(face_opposite[s] * 6, 5), at(face_offsets[s])))
    for s in range(4):
        messages.append(
            (pl.ds(s * 6 + 5, 1), pl.ds(edge_opposite[s] * 6 + 5, 1), at(edge_offsets[s]))
        )
    return messages


def kernel(
    steps, count_ref, face_len_ref, edge_len_ref,
    fwd_hbm, fwd_prev_hbm, adj_hbm, adj_prev_hbm, mass_hbm, ibool_hbm, jac_hbm, kap_hbm, mod_hbm,
    face_hbm, edge_hbm, rec_hbm, src_hbm, forward_hbm, backward_hbm, weight_hbm,
    packed,
    fwd_ref, fwd_prev_ref, adj_ref, adj_prev_ref, mass_ref, ibool_ref, jac_ref, kap_ref, mod_ref,
    face_ref, edge_ref, rec_ref, src_ref, forward_op, backward_op, weight_ref,
    now, prev, density, index, list_index, hot, row_hot, list_hot, list_row, table, points,
    bulk, shear, rhs, grad, flux, force, masked, total, kappa_sum, mu_sum, send, recv,
    in_sem, send_sem, recv_sem,
):
    arrivals = []
    for source, target in (
        (ibool_hbm, ibool_ref), (face_hbm, face_ref), (edge_hbm, edge_ref), (fwd_hbm, fwd_ref),
        (adj_hbm, adj_ref), (fwd_prev_hbm, fwd_prev_ref), (adj_prev_hbm, adj_prev_ref),
        (kap_hbm, kap_ref), (mod_hbm, mod_ref), (jac_hbm, jac_ref), (weight_hbm, weight_ref),
        (forward_hbm, forward_op), (backward_hbm, backward_op), (rec_hbm, rec_ref),
        (src_hbm, src_ref), (mass_hbm, mass_ref),
    ):
        copy = pltpu.make_async_copy(source, target, in_sem.at[len(arrivals)])
        copy.start()
        arrivals.append(copy)

    messages = partners()
    barrier = pltpu.get_barrier_semaphore()
    for _, _, device in messages:
        pl.semaphore_signal(barrier, inc=1, device_id=device, device_id_type=MESH)

    lane = lax.broadcasted_iota(jnp.int32, (1, LANES), 1)
    keep = jnp.where(lane < count_ref[0], 1.0, 0.0).astype(F32)
    index[...] = jnp.full((POINT_ROWS, LANES), -1, jnp.int32)
    list_index[...] = jnp.full((LIST_ROWS, LANES), -1, jnp.int32)
    bulk[...] = jnp.zeros((POINT_ROWS, LANES), F32)
    shear[...] = jnp.zeros((POINT_ROWS, LANES), F32)
    density[...] = jnp.zeros((64, LANES), F32)
    kappa_sum[...] = jnp.zeros((POINT_ROWS, LANES), F32)
    mu_sum[...] = jnp.zeros((POINT_ROWS, LANES), F32)
    send[...] = jnp.zeros(send.shape, F32)

    arrivals[0].wait()
    index[0:125, :] = ibool_ref[...]
    build_one_hot(index, POINT_ROWS, hot, row_hot)
    for copy in arrivals[1:]:
        copy.wait()

    width = edge_ref.shape[2]
    narrow = lax.broadcasted_iota(jnp.int32, (1, width), 1)
    for s in range(4):
        for k in range(5):
            nodes = face_ref[0, s : s + 1, k * LANES : (k + 1) * LANES]
            live = lane + k * LANES < face_len_ref[0, s]
            list_index[s * 6 + k : s * 6 + k + 1, :] = jnp.where(live, nodes, -1)
        nodes = edge_ref[0, s : s + 1, :]
        live = narrow < edge_len_ref[0, s]
        list_index[s * 6 + 5 : s * 6 + 6, 0:width] = jnp.where(live, nodes, -1)
    build_one_hot(list_index, LIST_ROWS, list_hot, list_row)
    bulk[0:125, :] = kap_ref[...]
    shear[0:125, :] = mod_ref[...]

    def spread(r, carry):
        at = pl.ds(pl.multiple_of(r * LANES, LANES), LANES)
        for base, target, source in (
            (0, now, fwd_ref), (3, now, adj_ref), (0, prev, fwd_prev_ref), (3, prev, adj_prev_ref),
        ):
            value = source[:, at]
            for c in range(3):
                target[base + c, pl.ds(r, 1), :] = value[c : c + 1]
        return carry

    lax.fori_loop(0, 64, spread, 0, unroll=8)

    element = lax.broadcasted_iota(jnp.int32, (LANES, LANES), 0)
    chosen = jnp.where(
        jnp.broadcast_to(rec_ref[...], (LANES, LANES)) == element, 1.0, 0.0
    ).astype(BF16)

    def put_point(i, c, value):
        points[c, pl.ds(pl.multiple_of(i * GROUP, GROUP), GROUP), :] = value

    scales = [jac_ref[d : d + 1, :] for d in range(3)]
    pl.semaphore_wait(barrier, len(messages))

    def one_step(step, carry):
        make_table(lambda c: now[c], FIELDS, table)
        gather(table, FIELDS, POINT_ROWS, GATHER_ROWS, hot, row_hot, put_point)
        element_force(
            points, bulk, shear, weight_ref, scales, keep, forward_op, backward_op,
            rhs, grad, flux, force,
        )
        for c in range(3):
            source = src_ref[c, pl.ds(step, 1), :]
            high, low = split(source)
            rest = source - high.astype(F32) - low.astype(F32)
            stack = jnp.concatenate(
                [
                    jnp.broadcast_to(part.astype(F32), (8, LANES))
                    for part in (high, low, rest)
                ],
                0,
            ).astype(BF16)
            found = lax.dot_general(
                stack, chosen, (((1,), (1,)), ((), ())), preferred_element_type=F32
            )
            lanes = slice((3 + c) * LANES, (4 + c) * LANES)
            force[62:63, lanes] += found[0:1] + found[8:9] + found[16:17]

        def load_point(i):
            at = pl.ds(pl.multiple_of(i * GROUP, GROUP), GROUP)
            blocks = [split(force[at, c * LANES : (c + 1) * LANES]) for c in range(FIELDS)]
            return lambda u, c: [part[u : u + 1] for part in blocks[c]]

        total[...] = jnp.zeros((TABLE, COLUMNS), F32)
        scatter(load_point, POINT_ROWS, SCATTER_ROWS, hot, row_hot, masked, total)
        high, low = split(total[...])
        table[:TABLE, :] = high
        table[TABLE:, :] = low

        def put_list(i, c, value):
            for u in range(GROUP):
                send[step, i * GROUP + u, c : c + 1, :] = value[u : u + 1]

        gather(table, FIELDS, LIST_ROWS, LIST_ROWS, list_hot, list_row, put_list)

        copies = []
        for slot, (source, target, device) in enumerate(messages):
            landing = face_opposite[slot] if slot < 4 else 4 + edge_opposite[slot - 4]
            copy = pltpu.make_async_remote_copy(
                src_ref=send.at[step, source],
                dst_ref=recv.at[step, target],
                send_sem=send_sem.at[step, slot],
                recv_sem=recv_sem.at[step, landing],
                device_id=device,
                device_id_type=MESH,
            )
            copy.start()
            copies.append(copy)
        add_moduli_kernels(grad, scales, keep, kappa_sum, mu_sum)
        for copy in copies:
            copy.wait_recv()

        def load_list(i):
            blocks = [split(recv[step, i * GROUP + u]) for u in range(GROUP)]
            return lambda u, c: [part[c : c + 1] for part in blocks[u]]

        scatter(load_list, LIST_ROWS, LIST_ROWS, list_hot, list_row, masked, total)

        for b in range(2):
            part = pl.ds(b * HIGH_ROWS, HIGH_ROWS)
            lanes = slice(b * LANES, (b + 1) * LANES)
            mass = mass_ref[part, :]
            accel = [
                mass * total[c * HIGH_ROWS : (c + 1) * HIGH_ROWS, lanes] for c in range(FIELDS)
            ]
            both = 0.0
            for c in range(3):
                both = both + accel[3 + c] * now[c, part, :]
            density[part, :] += time_step * both
            for c in range(FIELDS):
                field = now[c, part, :]
                later = 2.0 * field - prev[c, part, :] + time_step * time_step * accel[c]
                prev[c, part, :] = field
                now[c, part, :] = later
        for copy in copies:
            copy.wait_send()
        return carry

    lax.fori_loop(0, steps, one_step, 0)

    make_table(lambda c: density[...], 1, table)
    gather(table, 1, POINT_ROWS, GATHER_ROWS, hot, row_hot, put_point)
    for c in range(FIELDS):
        packed[c * 64 : (c + 1) * 64, :] = now[c]
    for k, value in enumerate((points[0] * keep, kappa_sum[...], mu_sum[...])):
        packed[FIELDS * 64 + k * POINT_ROWS : FIELDS * 64 + (k + 1) * POINT_ROWS, :] = value


def unpack(
    packed, fwd_out, adj_out, rho_out, kappa_out, mu_out, fwd, adj, rho, kappa, mu, out_sem
):
    copies = []
    for k, (source, target) in enumerate(((rho, rho_out), (kappa, kappa_out), (mu, mu_out))):
        top = FIELDS * 64 + k * POINT_ROWS
        source[...] = packed[top : top + 125, :]
        copies.append(pltpu.make_async_copy(source, target, out_sem.at[k]))
        copies[k].start()
    for k, (source, target) in enumerate(((fwd, fwd_out), (adj, adj_out))):
        for c in range(3):

            def join(i, carry):
                top = (k * 3 + c) * 64 + i * GROUP
                rows = packed[pl.ds(pl.multiple_of(top, GROUP), GROUP), :]
                for u in range(GROUP):
                    at = pl.ds(pl.multiple_of(i * WIDE + u * LANES, LANES), LANES)
                    source[c : c + 1, at] = rows[u : u + 1]
                return carry

            lax.fori_loop(0, 64 // GROUP, join, 0)
        copies.append(pltpu.make_async_copy(source, target, out_sem.at[3 + k]))
        copies[3 + k].start()
    for copy in copies:
        copy.wait()


def on_device(
    fwd_now, fwd_prev, adj_now, adj_prev, inv_mass, ibool, inv_jac, kappa, mu, elem_count,
    face_nodes, face_len, edge_nodes, edge_len, rec_elem, adj_src,
):
    forward_op, backward_op, weight = operators()
    steps = adj_src.shape[0]
    nodes = fwd_now.shape[1]
    elements = ibool.shape[1]
    vmem = pl.BlockSpec(memory_space=pltpu.VMEM)
    smem = pl.BlockSpec(memory_space=pltpu.SMEM)
    spread = POINT_ROWS * LANES
    listed = LIST_ROWS * LANES
    operands = (
        fwd_now, fwd_prev, adj_now, adj_prev, inv_mass.reshape(64, LANES), ibool, inv_jac, kappa, mu,
        face_nodes, edge_nodes, rec_elem.reshape(1, elements), adj_src.transpose(1, 0, 2),
        forward_op, backward_op, weight,
    )
    scratch = [pltpu.VMEM(operand.shape, operand.dtype) for operand in operands] + [
        pltpu.VMEM((FIELDS, 64, LANES), F32),
        pltpu.VMEM((FIELDS, 64, LANES), F32),
        pltpu.VMEM((64, LANES), F32),
        pltpu.VMEM((POINT_ROWS, LANES), jnp.int32),
        pltpu.VMEM((LIST_ROWS, LANES), jnp.int32),
        pltpu.VMEM((COLUMNS, spread), BF16),
        pltpu.VMEM((HIGH_ROWS, spread), BF16),
        pltpu.VMEM((COLUMNS, listed), BF16),
        pltpu.VMEM((HIGH_ROWS, listed), BF16),
        pltpu.VMEM((2 * TABLE, COLUMNS), BF16),
        pltpu.VMEM((FIELDS, POINT_ROWS, LANES), F32),
        pltpu.VMEM((POINT_ROWS, LANES), F32),
        pltpu.VMEM((POINT_ROWS, LANES), F32),
        pltpu.VMEM((384, FIELDS * LANES), BF16),
        pltpu.VMEM((384, FIELDS * LANES), F32),
        pltpu.VMEM((3 * 384, FIELDS * LANES), BF16),
        pltpu.VMEM((POINT_ROWS, FIELDS * LANES), F32),
        pltpu.VMEM((2 * TABLE, SCATTER_ROWS * LANES), BF16),
        pltpu.VMEM((TABLE, COLUMNS), F32),
        pltpu.VMEM((POINT_ROWS, LANES), F32),
        pltpu.VMEM((POINT_ROWS, LANES), F32),
        pltpu.VMEM((steps, LIST_ROWS, 8, LANES), F32),
        pltpu.VMEM((steps, LIST_ROWS, 8, LANES), F32),
        pltpu.SemaphoreType.DMA((len(operands),)),
        pltpu.SemaphoreType.DMA((steps, 8)),
        pltpu.SemaphoreType.DMA((steps, 8)),
    ]
    point = jax.ShapeDtypeStruct((125, elements), F32)
    node = jax.ShapeDtypeStruct((3, nodes), F32)
    hbm = pl.BlockSpec(memory_space=pl.ANY)
    packed = pl.pallas_call(
        functools.partial(kernel, steps),
        out_shape=jax.ShapeDtypeStruct((FIELDS * 64 + 3 * POINT_ROWS, LANES), F32),
        in_specs=[smem] * 3 + [hbm] * len(operands),
        out_specs=vmem,
        scratch_shapes=scratch,
        compiler_params=pltpu.CompilerParams(
            collective_id=0, has_side_effects=True, vmem_limit_bytes=60 << 20
        ),
    )(elem_count, face_len, edge_len, *operands)
    outs = (node, node, point, point, point)
    return pl.pallas_call(
        unpack,
        out_shape=outs,
        in_specs=[vmem],
        out_specs=(hbm,) * 5,
        scratch_shapes=[pltpu.VMEM(out.shape, F32) for out in outs]
        + [pltpu.SemaphoreType.DMA((len(outs),))],
        compiler_params=pltpu.CompilerParams(vmem_limit_bytes=60 << 20),
    )(packed)


def solution(mesh):
    field = P(None, ("row", "col"))
    part = P(("row", "col"))
    in_specs = (
        field, field, field, field, part, field, field, field, field, part,
        P(("row", "col"), None, None), P(("row", "col"), None),
        P(("row", "col"), None, None), P(("row", "col"), None),
        part, P(None, None, ("row", "col")),
    )
    return jax.shard_map(
        on_device, mesh=mesh, in_specs=in_specs, out_specs=(field,) * 5, check_vma=False
    )
```

time: 89.5 us -> 63.8 us (0.71)
  local copies, waits for them, and re-layouts: 15.5 us -> 0 us
  Pallas kernels: 71.9 us -> 61.5 us
    unnamed x40 -> x0, local copies, waits for them, and re-layouts: 15.5 us -> none
    pallas_call x1 -> x2, Pallas kernels: 71.9 us -> 61.5 us  [the longest x1 59.1 us: on_device(): pl.pallas_call(functools.partial(kernel, steps), out_shape=jax.ShapeDtype...]
where the time goes in v2:
time: 63.8 us; the launch traced here: 62.8 us
  Pallas kernels  61.5 us (96%)
  between operations  1.29 us (2%)
    pallas_call x1, Pallas kernels, on_device(): pl.pallas_call(functools.partial(kernel, steps), out_shape=jax.ShapeDtype...  59.1 us
    pallas_call x1, Pallas kernels, on_device(): pl.pallas_call(unpack, out_shape=outs, in_specs=[vmem], out_specs=(hbm,)...  2.37 us

profile of v2, /device:TPU:1, one launch (start us, length us, event | category | flops | bytes accessed | tf_op | source)
XLA Modules:
  0.0 62.8 jit_solution(17598874887751762384)
XLA Ops:
  1.3 59.1 %shard_map.218.packed = f32[768,128]{1,0:T(8,128)} custom-call(s32[1]{0:T(128)S(6)} %copy.24.count_ref, s32[1,4]{1,0:T(1,128)} %face_len_ref.1, s32[1,4]{1,0:T(1,128)} %edge_len_ref.1, f32[3,8192]{1,0:T(4,128)} %fwd_hbm.1, f32[3,8192]{1,0:T(4,128)} %fwd_prev_hbm.1, f32[3,8192]{1,0:T(4,128)} %adj_hbm.1, f32[3,8192]{1,0:T(4,128)} %adj_prev_hbm.1, ...), custom_call_target="tpu_custom_call" | custom-call | tf_op jit(solution)/shard_map/pallas_call | solution.py:537
  60.4 2.4 %shard_map.219 = (f32[3,8192]{1,0:T(4,128)}, f32[3,8192]{1,0:T(4,128)}, f32[125,128]{1,0:T(8,128)}, f32[125,128]{1,0:T(8,128)}, f32[125,128]{1,0:T(8,128)}) custom-call(f32[768,128]{1,0:T(8,128)} %shard_map.218.packed), custom_call_target="tpu_custom_call" | custom-call | tf_op jit(solution)/shard_map/pallas_call | solution.py:548

commit v3 on v2

--- a/solution.py
+++ b/solution.py
@@ -24,7 +24,7 @@
 LIST_ROWS = 24
 GROUP = 8
 WIDE = GROUP * LANES
-GATHER_ROWS = 64
+GATHER_ROWS = 128
 SCATTER_ROWS = 64
 
 face_offsets = ((0, 1), (0, -1), (1, 0), (-1, 0))
@@ -98,7 +98,7 @@
             row_ref[:, at] = jnp.where(here, one, zero)
         return carry
 
-    lax.fori_loop(0, rows // GROUP, body, 0)
+    lax.fori_loop(0, rows // GROUP, body, 0, unroll=2 if rows % 16 == 0 else 1)
 
 
 def make_table(source, fields, table_ref):
@@ -240,7 +240,7 @@
                             flux_ref[pl.ds(top, tile), lanes] = value
         return carry
 
-    lax.fori_loop(0, POINT_ROWS // 16, body, 0, unroll=4)
+    lax.fori_loop(0, POINT_ROWS // 16, body, 0, unroll=8)
     force_ref[...] = jnp.dot(backward_op[...], flux_ref[...], preferred_element_type=F32)
 
 
@@ -260,7 +260,7 @@
         mu_ref[at, :] += 2.0 * time_step * (even + 2.0 * odd) * keep
         return carry
 
-    lax.fori_loop(0, POINT_ROWS // 16, body, 0, unroll=4)
+    lax.fori_loop(0, POINT_ROWS // 16, body, 0, unroll=8)
 
 
 def partners():
@@ -284,10 +284,11 @@
 
 
 def kernel(
-    steps, count_ref, face_len_ref, edge_len_ref,
+    steps, count_hbm, face_len_hbm, edge_len_hbm,
     fwd_hbm, fwd_prev_hbm, adj_hbm, adj_prev_hbm, mass_hbm, ibool_hbm, jac_hbm, kap_hbm, mod_hbm,
     face_hbm, edge_hbm, rec_hbm, src_hbm, forward_hbm, backward_hbm, weight_hbm,
     packed,
+    count_ref, face_len_ref, edge_len_ref,
     fwd_ref, fwd_prev_ref, adj_ref, adj_prev_ref, mass_ref, ibool_ref, jac_ref, kap_ref, mod_ref,
     face_ref, edge_ref, rec_ref, src_ref, forward_op, backward_op, weight_ref,
     now, prev, density, index, list_index, hot, row_hot, list_hot, list_row, table, points,
@@ -296,7 +297,8 @@
 ):
     arrivals = []
     for source, target in (
-        (ibool_hbm, ibool_ref), (face_hbm, face_ref), (edge_hbm, edge_ref), (fwd_hbm, fwd_ref),
+        (ibool_hbm, ibool_ref), (count_hbm, count_ref), (face_len_hbm, face_len_ref),
+        (edge_len_hbm, edge_len_ref), (face_hbm, face_ref), (edge_hbm, edge_ref), (fwd_hbm, fwd_ref),
         (adj_hbm, adj_ref), (fwd_prev_hbm, fwd_prev_ref), (adj_prev_hbm, adj_prev_ref),
         (kap_hbm, kap_ref), (mod_hbm, mod_ref), (jac_hbm, jac_ref), (weight_hbm, weight_ref),
         (forward_hbm, forward_op), (backward_hbm, backward_op), (rec_hbm, rec_ref),
@@ -312,7 +314,6 @@
         pl.semaphore_signal(barrier, inc=1, device_id=device, device_id_type=MESH)
 
     lane = lax.broadcasted_iota(jnp.int32, (1, LANES), 1)
-    keep = jnp.where(lane < count_ref[0], 1.0, 0.0).astype(F32)
     index[...] = jnp.full((POINT_ROWS, LANES), -1, jnp.int32)
     list_index[...] = jnp.full((LIST_ROWS, LANES), -1, jnp.int32)
     bulk[...] = jnp.zeros((POINT_ROWS, LANES), F32)
@@ -328,15 +329,17 @@
     for copy in arrivals[1:]:
         copy.wait()
 
+    count = jnp.broadcast_to(count_ref[...], (1, LANES))
+    keep = jnp.where(lane < count, 1.0, 0.0).astype(F32)
     width = edge_ref.shape[2]
     narrow = lax.broadcasted_iota(jnp.int32, (1, width), 1)
     for s in range(4):
         for k in range(5):
             nodes = face_ref[0, s : s + 1, k * LANES : (k + 1) * LANES]
-            live = lane + k * LANES < face_len_ref[0, s]
+            live = lane + k * LANES < jnp.broadcast_to(face_len_ref[:, s : s + 1], (1, LANES))
             list_index[s * 6 + k : s * 6 + k + 1, :] = jnp.where(live, nodes, -1)
         nodes = edge_ref[0, s : s + 1, :]
-        live = narrow < edge_len_ref[0, s]
+        live = narrow < jnp.broadcast_to(edge_len_ref[:, s : s + 1], (1, width))
         list_index[s * 6 + 5 : s * 6 + 6, 0:width] = jnp.where(live, nodes, -1)
     build_one_hot(list_index, LIST_ROWS, list_hot, list_row)
     bulk[0:125, :] = kap_ref[...]
@@ -479,7 +482,7 @@
                     source[c : c + 1, at] = rows[u : u + 1]
                 return carry
 
-            lax.fori_loop(0, 64 // GROUP, join, 0)
+            lax.fori_loop(0, 64 // GROUP, join, 0, unroll=True)
         copies.append(pltpu.make_async_copy(source, target, out_sem.at[3 + k]))
         copies[3 + k].start()
     for copy in copies:
@@ -495,10 +498,10 @@
     nodes = fwd_now.shape[1]
     elements = ibool.shape[1]
     vmem = pl.BlockSpec(memory_space=pltpu.VMEM)
-    smem = pl.BlockSpec(memory_space=pltpu.SMEM)
     spread = POINT_ROWS * LANES
     listed = LIST_ROWS * LANES
     operands = (
+        elem_count.reshape(1, 1), face_len, edge_len,
         fwd_now, fwd_prev, adj_now, adj_prev, inv_mass.reshape(64, LANES), ibool, inv_jac, kappa, mu,
         face_nodes, edge_nodes, rec_elem.reshape(1, elements), adj_src.transpose(1, 0, 2),
         forward_op, backward_op, weight,
@@ -537,13 +540,13 @@
     packed = pl.pallas_call(
         functools.partial(kernel, steps),
         out_shape=jax.ShapeDtypeStruct((FIELDS * 64 + 3 * POINT_ROWS, LANES), F32),
-        in_specs=[smem] * 3 + [hbm] * len(operands),
+        in_specs=[hbm] * len(operands),
         out_specs=vmem,
         scratch_shapes=scratch,
         compiler_params=pltpu.CompilerParams(
             collective_id=0, has_side_effects=True, vmem_limit_bytes=60 << 20
         ),
-    )(elem_count, face_len, edge_len, *operands)
+    )(*operands)
     outs = (node, node, point, point, point)
     return pl.pallas_call(
         unpack,

time: 63.8 us -> 61.2 us (0.959)
  Pallas kernels: 61.5 us -> 58.9 us
    pallas_call x1, Pallas kernels: 59.1 us -> 57.1 us  [on_device(): pl.pallas_call(functools.partial(kernel, steps), out_shape=jax.ShapeDtype...]
where the time goes in v3:
time: 61.2 us; the launch traced here: 60.2 us
  Pallas kernels  58.9 us (96%)
  between operations  1.29 us (2%)
    pallas_call x1, Pallas kernels, on_device(): pl.pallas_call(functools.partial(kernel, steps), out_shape=jax.ShapeDtype...  57.1 us
    pallas_call x1, Pallas kernels, on_device(): pl.pallas_call(unpack, out_shape=outs, in_specs=[vmem], out_specs=(hbm,)...  1.81 us

profile of v3, /device:TPU:1, one launch (start us, length us, event | category | flops | bytes accessed | tf_op | source)
XLA Modules:
  0.0 60.2 jit_solution(8728061026398184192)
XLA Ops:
  1.3 57.1 %shard_map.218.packed = f32[768,128]{1,0:T(8,128)} custom-call(s32[1,1]{1,0:T(1,128)} %bitcast.4.count_hbm, s32[1,4]{1,0:T(1,128)} %face_len_hbm.1, s32[1,4]{1,0:T(1,128)} %edge_len_hbm.1, f32[3,8192]{1,0:T(4,128)} %fwd_hbm.1, f32[3,8192]{1,0:T(4,128)} %fwd_prev_hbm.1, f32[3,8192]{1,0:T(4,128)} %adj_hbm.1, f32[3,8192]{1,0:T(4,128)} %adj_prev_hbm.1, ...), custom_call_target="tpu_custom_call" | custom-call | tf_op jit(solution)/shard_map/pallas_call | solution.py:540
  58.4 1.8 %shard_map.219 = (f32[3,8192]{1,0:T(4,128)}, f32[3,8192]{1,0:T(4,128)}, f32[125,128]{1,0:T(8,128)}, f32[125,128]{1,0:T(8,128)}, f32[125,128]{1,0:T(8,128)}) custom-call(f32[768,128]{1,0:T(8,128)} %shard_map.218.packed), custom_call_target="tpu_custom_call" | custom-call | tf_op jit(solution)/shard_map/pallas_call | solution.py:551
